TPU v7x, 32 devices: a whole 2x2x4 slice. The times are simulated.
32 devices in a mesh: box: 16 (over z, y, x), tile: 2 (over core).
Axes of the slice: x: 2, y: 2, z: 4, core: 2. Of those that a mesh axis runs over, the one named last changes fastest.
Arguments:
- atom_pos: bfloat16 [3, 16384], P(None, ('box', 'tile')), may hold values from 0 to 12
- atom_feat: bfloat16 [16384, 256], P(('box', 'tile')), may hold values from -6 to 6
- tile_cells: int32 [32], P(('box', 'tile')), may hold values from 0 to 1, as said below
- atom_pairs: int32 [128, 6], P(('box', 'tile')), may hold values from 0 to 35, as said below
- atom_counts: int32 [128], P(('box', 'tile')), may hold values from 1 to 6, as said below
- probe_pos: bfloat16 [3, 16384], P(None, ('box', 'tile')), may hold values from 0 to 12
- probe_pairs: int32 [128, 4], P(('box', 'tile')), may hold values from 0 to 35, as said below
- probe_counts: int32 [128], P(('box', 'tile')), may hold values from 1 to 4, as said below
- filt_atom: bfloat16 [20, 256], replicated, may hold values from -1.25 to 1.25
- upd_first: bfloat16 [256, 256], replicated, may hold values from -0.375 to 0.375
- upd_second: bfloat16 [256, 256], replicated, may hold values from -0.375 to 0.375
- filt_probe: bfloat16 [20, 256], replicated, may hold values from -1.25 to 1.25
- read_first: bfloat16 [256, 256], replicated, may hold values from -0.375 to 0.375
- read_out: bfloat16 [256], replicated, may hold values from -0.375 to 0.375
Outputs:
- atom_out: bfloat16 [16384, 256], P(('box', 'tile'))
- density: float32 [16384], P(('box', 'tile'))
Inputs may be any that keep to these rules, and one draw needn't show every extreme that they name: `tile_cells`: each run of 2 entries that belongs to one box index holds every z slab number exactly once. `atom_pairs`: each row holds 6 different source block numbers of the atom window. `atom_counts`: at least one entry over all cells equals 6. `probe_pairs`: each row holds 4 different source block numbers of the atom window. `probe_counts`: at least one entry over all cells equals 4.
All inputs are finite; a program needn't handle non-finite values.
Results may differ from a plain program's by a relative error of at most 0.0069.
Values may be sent and summed in bfloat16 or wider, within the bound.
A program may use at most 64 MiB of HBM per device.

v0:
```python
import functools
import math

import jax
import jax.numpy as jnp
from jax import lax
from jax.experimental import pallas as pl
from jax.experimental.pallas import tpu as pltpu
from jax.sharding import PartitionSpec as P

BLOCK = 128
CELL = 12.0
CUTOFF = 5.0
VMEM_LIMIT = 48 * 1024 * 1024


def shifted_softplus(v):
    return jnp.maximum(v, 0.0) + jnp.log1p(jnp.exp(-jnp.abs(v))) - math.log(2.0)


def halo(mine, count):
    tail = lax.ppermute(mine, "box", [(i, (i + 1) % count) for i in range(count)])
    head = lax.ppermute(mine, "box", [((i + 1) % count, i) for i in range(count)])
    return jnp.concatenate([tail, mine, head], axis=0)


def spread_filter(filt_ref, wide_ref):
    count = filt_ref.shape[0]
    mid = count // 2
    filt = filt_ref[...].astype(jnp.float32)
    for r in range(count):
        row = filt[r : r + 1, :] * math.exp(-0.5 * (r - mid) ** 2)
        wide_ref[r] = jnp.broadcast_to(row, wide_ref.shape[1:]).astype(jnp.bfloat16)


def basis_terms(tx, ty, tz, sx, sy, sz, count, self_flag):
    dx, dy, dz = tx - sx, ty - sy, tz - sz
    square = dx * dx + dy * dy + dz * dz
    inside = square < CUTOFF * CUTOFF
    if self_flag is not None:
        rows = lax.broadcasted_iota(jnp.int32, square.shape, 0)
        cols = lax.broadcasted_iota(jnp.int32, square.shape, 1)
        inside = jnp.logical_and(inside, rows - cols != self_flag)
    square = jnp.minimum(square, CUTOFF * CUTOFF)
    angle = square * (math.pi / (2.0 * CUTOFF)) ** 2
    cosine = jnp.full_like(angle, 1.0 / math.factorial(12))
    for n in (10, 8, 6, 4, 2, 0):
        cosine = cosine * angle + (-1.0) ** (n // 2) / math.factorial(n)
    mid = count // 2
    ratio = jnp.sqrt(square) * ((count - 1) / CUTOFF) - mid
    middle = jnp.where(inside, cosine * cosine * jnp.exp(-0.5 * ratio * ratio), 0.0)
    up, down = jnp.exp(ratio), jnp.exp(-ratio)
    terms = [None] * count
    terms[mid] = middle
    for r in range(mid + 1, count):
        terms[r] = terms[r - 1] * up
    for r in range(mid - 1, -1, -1):
        terms[r] = terms[r + 1] * down
    return [t.astype(jnp.bfloat16) for t in terms]


def gather_messages(block, slab, tiles, pairs, counts, target, pos, feat, wide, acc, self_check):
    nb = pairs.shape[0]
    cols = [
        jnp.broadcast_to(target[block, n : n + 1, :], (BLOCK, BLOCK)).T for n in range(3)
    ]
    acc[...] = jnp.zeros_like(acc)

    def slot(k, carry):
        q = pairs[block, k]
        cell = q // nb
        step_x, step_z = cell // 3, lax.rem(cell, 3)
        near = lax.rem(slab + step_z + (tiles - 1), tiles)
        where = (step_x * tiles + near) * nb + lax.rem(q, nb)
        shift_x = (step_x - 1).astype(jnp.float32) * CELL
        shift_z = (step_z - 1).astype(jnp.float32) * CELL
        flag = None
        if self_check:
            flag = jnp.where(q == 4 * nb + block, 0, 2 * BLOCK)
        spot = pos[where]
        terms = basis_terms(
            *cols,
            spot[0:1, :] + shift_x,
            spot[1:2, :],
            spot[2:3, :] + shift_z,
            wide.shape[0],
            flag,
        )
        source = feat[where].reshape(BLOCK // 16, 16, feat.shape[-1])
        scaled = [
            (source * wide[r][None]).reshape(BLOCK, feat.shape[-1]) for r in range(wide.shape[0])
        ]
        acc[...] += jnp.dot(
            jnp.concatenate(terms, axis=1),
            jnp.concatenate(scaled, axis=0),
            preferred_element_type=jnp.float32,
        )
        return carry

    lax.fori_loop(0, counts[block], slot, 0)


def atom_kernel(
    tiles, pairs, counts, slab, target, pos, feat, filt, first, second, own, out, wide, acc
):
    spread_filter(filt, wide)
    def each(block, carry):
        gather_messages(
            block, slab[0], tiles, pairs, counts, target, pos, feat, wide, acc, True
        )
        hidden = shifted_softplus(
            jnp.dot(
                acc[...].astype(jnp.bfloat16), first[...], preferred_element_type=jnp.float32
            )
        ).astype(jnp.bfloat16)
        change = jnp.dot(hidden, second[...], preferred_element_type=jnp.float32)
        out[block] = (own[block].astype(jnp.float32) + change).astype(jnp.bfloat16)
        return carry

    lax.fori_loop(0, pairs.shape[0], each, 0)


def probe_kernel(
    tiles, pairs, counts, slab, target, pos, feat, filt, first, last, out, wide, acc
):
    spread_filter(filt, wide)
    def each(block, carry):
        gather_messages(
            block, slab[0], tiles, pairs, counts, target, pos, feat, wide, acc, False
        )
        hidden = shifted_softplus(
            jnp.dot(
                acc[...].astype(jnp.bfloat16), first[...], preferred_element_type=jnp.float32
            )
        ).astype(jnp.bfloat16)
        lifted = hidden.astype(jnp.float32) * last[...].astype(jnp.float32)
        out[block] = jnp.sum(lifted.T, axis=0, keepdims=True)
        return carry

    lax.fori_loop(0, pairs.shape[0], each, 0)


def shards(
    tiles,
    boxes,
    atom_pos,
    atom_feat,
    tile_cells,
    atom_pairs,
    atom_counts,
    probe_pos,
    probe_pairs,
    probe_counts,
    filt_atom,
    upd_first,
    upd_second,
    filt_probe,
    read_first,
    read_out,
):
    atoms, width = atom_feat.shape
    nb = atoms // BLOCK
    count = filt_atom.shape[0]

    def blocks_of(pos):
        return pos.reshape(3, -1, BLOCK).transpose(1, 0, 2).astype(jnp.float32)

    def columns(mine):
        column = lax.all_gather(mine, "tile", axis=0, tiled=True)
        return halo(column, boxes)

    smem = pl.BlockSpec(memory_space=pltpu.SMEM)
    vmem = pl.BlockSpec(memory_space=pltpu.VMEM)
    scratch = [
        pltpu.VMEM((count, 16, width), jnp.bfloat16),
        pltpu.VMEM((BLOCK, width), jnp.float32),
    ]
    params = pltpu.CompilerParams(vmem_limit_bytes=VMEM_LIMIT)
    own_pos = blocks_of(atom_pos)
    own_feat = atom_feat.reshape(nb, BLOCK, width)
    pos = columns(own_pos)
    here = lax.axis_index("tile").astype(jnp.int32).reshape(1)
    fresh = pl.pallas_call(
        functools.partial(atom_kernel, tiles),
        out_shape=jax.ShapeDtypeStruct((nb, BLOCK, width), jnp.bfloat16),
        in_specs=[smem] * 3 + [vmem] * 7,
        out_specs=vmem,
        scratch_shapes=scratch,
        compiler_params=params,
    )(
        atom_pairs,
        atom_counts,
        here,
        own_pos,
        pos,
        columns(own_feat),
        filt_atom,
        upd_first,
        upd_second,
        own_feat,
    )
    probe_blocks = blocks_of(probe_pos)
    density = pl.pallas_call(
        functools.partial(probe_kernel, tiles),
        out_shape=jax.ShapeDtypeStruct((probe_blocks.shape[0], 1, BLOCK), jnp.float32),
        in_specs=[smem] * 3 + [vmem] * 6,
        out_specs=vmem,
        scratch_shapes=scratch,
        compiler_params=params,
    )(
        probe_pairs,
        probe_counts,
        tile_cells,
        probe_blocks,
        pos,
        columns(fresh),
        filt_probe,
        read_first,
        read_out.reshape(1, width),
    )
    return (fresh.reshape(atoms, width), density.reshape(-1))


def solution(mesh):
    both = ("box", "tile")
    placed = (
        P(None, both),
        P(both, None),
        P(both),
        P(both, None),
        P(both),
        P(None, both),
        P(both, None),
        P(both),
    ) + (P(),) * 6
    return jax.shard_map(
        functools.partial(shards, mesh.shape["tile"], mesh.shape["box"]),
        mesh=mesh,
        in_specs=placed,
        out_specs=(P(both, None), P(both)),
        check_vma=False,
    )
```

profile of v0, /device:TPU:0, one launch (start us, length us, event | category | flops | bytes accessed | tf_op | source)
XLA Modules:
  0.0 78.7 jit_solution(3987169571465331404)
XLA Ops:
  0.6 2.5 %all_gather.10 = bf16[8,128,256]{2,1,0:T(8,128)(2,1)S(1)} all-gather(bf16[4,128,256]{2,1,0:T(8,128)(2,1)} %bitcast.14), channel_id=1, replica_groups=mesh['box'=16,'tile'=2] {'tile'}, dimensions={0}, use_global_device_ids=true | all-gather | bytes 786432 | tf_op jit(solution)/shard_map/all_gather | solution.py:169
  3.1 2.9 %collective-permute-start.2 = (bf16[8,128,256]{2,1,0:T(8,128)(2,1)S(1)}, bf16[8,128,256]{2,1,0:T(8,128)(2,1)S(1)}, u32[]{:S(2)}, u32[]{:S(2)}) collective-permute-start(bf16[8,128,256]{2,1,0:T(8,128)(2,1)S(1)} %all_gather.10), channel_id=1, source_target_pairs={{0,2},{2,4},{4,6},{6,8},{8,10},{10,12},{12,14},{14,16},{16,18},{18... | collective-permute-start | bytes 1572872 | tf_op jit(solution)/shard_map/ppermute | solution.py:22
  6.0 4.0 %collective-permute-start.3 = (bf16[8,128,256]{2,1,0:T(8,128)(2,1)S(1)}, bf16[8,128,256]{2,1,0:T(8,128)(2,1)S(1)}, u32[]{:S(2)}, u32[]{:S(2)}) collective-permute-start(bf16[8,128,256]{2,1,0:T(8,128)(2,1)S(1)} %all_gather.10), channel_id=1, source_target_pairs={{2,0},{4,2},{6,4},{8,6},{10,8},{12,10},{14,12},{16,14},{18,16},{20... | collective-permute-start | bytes 1572872 | tf_op jit(solution)/shard_map/ppermute | solution.py:23
  10.0 0.7 convert_bitcast_fusion.1.target
  10.6 1.8 %all_gather.9 = f32[8,3,128]{2,1,0:T(4,128)S(1)} all-gather(f32[4,3,128]{2,1,0:T(4,128)S(1)} %convert_bitcast_fusion.1.target), channel_id=1, replica_groups=mesh['box'=16,'tile'=2] {'tile'}, dimensions={0}, use_global_device_ids=true | all-gather | bytes 18432 | tf_op jit(solution)/shard_map/all_gather | solution.py:169
  12.5 0.0 collective-permute-start
  12.5 5.6 %collective-permute-start.1 = (f32[8,3,128]{2,1,0:T(4,128)S(1)}, f32[8,3,128]{2,1,0:T(4,128)S(1)}, u32[]{:S(2)}, u32[]{:S(2)}) collective-permute-start(f32[8,3,128]{2,1,0:T(4,128)S(1)} %all_gather.9), channel_id=1, source_target_pairs={{2,0},{4,2},{6,4},{8,6},{10,8},{12,10},{14,12},{16,14},{18,16},{20... | collective-permute-start | bytes 36872 | tf_op jit(solution)/shard_map/ppermute | solution.py:23
  18.1 11.3 %collective-permute-done = f32[8,3,128]{2,1,0:T(4,128)S(1)} collective-permute-done((f32[8,3,128]{2,1,0:T(4,128)S(1)}, f32[8,3,128]{2,1,0:T(4,128)S(1)}, u32[]{:S(2)}, u32[]{:S(2)}) %collective-permute-start) | collective-permute-done | bytes 12320 | tf_op jit(solution)/shard_map/ppermute | solution.py:22
  29.4 1.9 %collective-permute-done.1 = f32[8,3,128]{2,1,0:T(4,128)S(1)} collective-permute-done((f32[8,3,128]{2,1,0:T(4,128)S(1)}, f32[8,3,128]{2,1,0:T(4,128)S(1)}, u32[]{:S(2)}, u32[]{:S(2)}) %collective-permute-start.1) | collective-permute-done | bytes 12320 | tf_op jit(solution)/shard_map/ppermute | solution.py:23
  31.3 0.0 copy-start
  31.3 0.0 copy-start.1
  31.4 0.0 copy-start.2
  31.4 0.0 copy-start.4
  31.4 0.0 copy-start.6
  31.4 0.0 copy-start.8
  31.4 0.0 collective-permute-done.2
  31.4 0.0 collective-permute-done.3
  31.4 0.2 pad_maximum_fusion.feat
  31.6 0.7 copy-done
  32.3 0.0 copy-done.1
  32.3 0.1 copy-done.2
  32.4 0.0 copy-done.4
  32.4 0.0 copy-done.6
  32.4 0.0 copy-done.8
  32.4 0.0 copy-start.11
  32.4 0.0 copy-start.10
  32.4 7.6 %shard_map.149 = bf16[4,128,256]{2,1,0:T(8,128)(2,1)} custom-call(s32[4,6]{1,0:T(4,128)S(1)} %copy-done.6, s32[4]{0:T(128)S(1)} %copy-done.8, s32[1]{0:T(128)} %bitcast.slab, f32[4,3,128]{2,1,0:T(4,128)S(1)} %convert_bitcast_fusion.1.target, f32[24,3,128]{2,1,0:T(4,128)S(1)} %constant_dynamic-update-slice_fusion.pos, ...), custom_call_target="tpu_custom_call" | custom-call | tf_op jit(solution)/shard_map/pallas_call | solution.py:183
  40.0 2.4 %all_gather.11 = bf16[8,128,256]{2,1,0:T(8,128)(2,1)S(1)} all-gather(bf16[4,128,256]{2,1,0:T(8,128)(2,1)} %shard_map.149), channel_id=1, replica_groups=mesh['box'=16,'tile'=2] {'tile'}, dimensions={0}, use_global_device_ids=true | all-gather | bytes 786432 | tf_op jit(solution)/shard_map/all_gather | solution.py:169
  42.4 0.0 collective-permute-start.4
  42.4 11.2 %collective-permute-start.5 = (bf16[8,128,256]{2,1,0:T(8,128)(2,1)S(1)}, bf16[8,128,256]{2,1,0:T(8,128)(2,1)S(1)}, u32[]{:S(2)}, u32[]{:S(2)}) collective-permute-start(bf16[8,128,256]{2,1,0:T(8,128)(2,1)S(1)} %all_gather.11), channel_id=1, source_target_pairs={{2,0},{4,2},{6,4},{8,6},{10,8},{12,10},{14,12},{16,14},{18,16},{20... | collective-permute-start | bytes 1572872 | tf_op jit(solution)/shard_map/ppermute | solution.py:23
  53.6 0.0 copy-done.11
  54.3 0.0 copy-done.10
  54.3 0.0 copy-start.3
  54.3 0.0 copy-start.5
  54.3 0.0 copy-start.7
  54.3 0.0 copy-start.9
  54.4 11.6 %collective-permute-done.4 = bf16[8,128,256]{2,1,0:T(8,128)(2,1)S(1)} collective-permute-done((bf16[8,128,256]{2,1,0:T(8,128)(2,1)S(1)}, bf16[8,128,256]{2,1,0:T(8,128)(2,1)S(1)}, u32[]{:S(2)}, u32[]{:S(2)}) %collective-permute-start.4) | collective-permute-done | bytes 524320 | tf_op jit(solution)/shard_map/ppermute | solution.py:22
  66.0 5.1 %collective-permute-done.5 = bf16[8,128,256]{2,1,0:T(8,128)(2,1)S(1)} collective-permute-done((bf16[8,128,256]{2,1,0:T(8,128)(2,1)S(1)}, bf16[8,128,256]{2,1,0:T(8,128)(2,1)S(1)}, u32[]{:S(2)}, u32[]{:S(2)}) %collective-permute-start.5) | collective-permute-done | bytes 524320 | tf_op jit(solution)/shard_map/ppermute | solution.py:23
  71.1 0.2 pad_maximum_fusion.1.feat
  71.3 0.0 copy-done.3
  71.3 0.0 copy-done.5
  71.3 0.0 copy-done.7
  71.3 0.0 copy-done.9
  71.3 7.3 %shard_map.150 = f32[4,1,128]{2,1,0:T(1,128)} custom-call(s32[4,4]{1,0:T(4,128)S(1)} %copy-done.7, s32[4]{0:T(128)S(1)} %copy-done.9, s32[1]{0:T(128)S(6)} %copy.18.slab, f32[4,3,128]{2,1,0:T(4,128)S(1)} %convert_bitcast_fusion.target, f32[24,3,128]{2,1,0:T(4,128)S(1)} %constant_dynamic-update-slice_fusion.pos, ...), custom_call_target="tpu_custom_call" | custom-call | tf_op jit(solution)/shard_map/pallas_call | solution.py:203
  (5 shorter events, 0.0 us)
Async XLA Ops:
  3.1 28.3 %collective-permute-start.2 = (bf16[8,128,256]{2,1,0:T(8,128)(2,1)S(1)}, bf16[8,128,256]{2,1,0:T(8,128)(2,1)S(1)}, u32[]{:S(2)}, u32[]{:S(2)}) collective-permute-start(bf16[8,128,256]{2,1,0:T(8,128)(2,1)S(1)} %all_gather.10), channel_id=1, source_target_pairs={{0,2},{2,4},{4,6},{6,8},{8,10},{10,12},{12,14},{14,16},{16,18},{18... | collective-permute-start | bytes 1572872 | tf_op jit(solution)/shard_map/ppermute | solution.py:22
  6.0 25.5 %collective-permute-start.3 = (bf16[8,128,256]{2,1,0:T(8,128)(2,1)S(1)}, bf16[8,128,256]{2,1,0:T(8,128)(2,1)S(1)}, u32[]{:S(2)}, u32[]{:S(2)}) collective-permute-start(bf16[8,128,256]{2,1,0:T(8,128)(2,1)S(1)} %all_gather.10), channel_id=1, source_target_pairs={{2,0},{4,2},{6,4},{8,6},{10,8},{12,10},{14,12},{16,14},{18,16},{20... | collective-permute-start | bytes 1572872 | tf_op jit(solution)/shard_map/ppermute | solution.py:23
  12.5 16.9 %collective-permute-start = (f32[8,3,128]{2,1,0:T(4,128)S(1)}, f32[8,3,128]{2,1,0:T(4,128)S(1)}, u32[]{:S(2)}, u32[]{:S(2)}) collective-permute-start(f32[8,3,128]{2,1,0:T(4,128)S(1)} %all_gather.9), channel_id=1, source_target_pairs={{0,2},{2,4},{4,6},{6,8},{8,10},{10,12},{12,14},{14,16},{16,18},{18... | collective-permute-start | bytes 36872 | tf_op jit(solution)/shard_map/ppermute | solution.py:22
  12.5 18.8 %collective-permute-start.1 = (f32[8,3,128]{2,1,0:T(4,128)S(1)}, f32[8,3,128]{2,1,0:T(4,128)S(1)}, u32[]{:S(2)}, u32[]{:S(2)}) collective-permute-start(f32[8,3,128]{2,1,0:T(4,128)S(1)} %all_gather.9), channel_id=1, source_target_pairs={{2,0},{4,2},{6,4},{8,6},{10,8},{12,10},{14,12},{16,14},{18,16},{20... | collective-permute-start | bytes 36872 | tf_op jit(solution)/shard_map/ppermute | solution.py:23
  31.3 1.0 %copy-start = (bf16[512,256]{1,0:T(8,128)(2,1)S(1)}, bf16[512,256]{1,0:T(8,128)(2,1)}, u32[]{:S(2)}) copy-start(bf16[512,256]{1,0:T(8,128)(2,1)} %param.15) | copy-start | bytes 786436
  31.3 1.0 %copy-start.1 = (bf16[256,256]{1,0:T(8,128)(2,1)S(1)}, bf16[256,256]{1,0:T(8,128)(2,1)}, u32[]{:S(2)}) copy-start(bf16[256,256]{1,0:T(8,128)(2,1)} %first.2) | copy-start | bytes 393220
  31.4 1.0 %copy-start.2 = (bf16[256,256]{1,0:T(8,128)(2,1)S(1)}, bf16[256,256]{1,0:T(8,128)(2,1)}, u32[]{:S(2)}) copy-start(bf16[256,256]{1,0:T(8,128)(2,1)} %second.1) | copy-start | bytes 393220
  31.4 1.0 %copy-start.4 = (bf16[20,256]{1,0:T(8,128)(2,1)S(1)}, bf16[20,256]{1,0:T(8,128)(2,1)}, u32[]{:S(2)}) copy-start(bf16[20,256]{1,0:T(8,128)(2,1)} %filt.2) | copy-start | bytes 30724
  31.4 1.0 %copy-start.6 = (s32[4,6]{1,0:T(4,128)S(1)}, s32[4,6]{1,0:T(4,128)}, u32[]{:S(2)}) copy-start(s32[4,6]{1,0:T(4,128)} %pairs.2) | copy-start | bytes 292
  31.4 1.0 %copy-start.8 = (s32[4]{0:T(128)S(1)}, s32[4]{0:T(128)}, u32[]{:S(2)}) copy-start(s32[4]{0:T(128)} %counts.2) | copy-start | bytes 52
  32.4 21.2 %copy-start.11 = (bf16[256]{0:T(256)(128)(2,1)S(1)}, bf16[256]{0:T(256)(128)(2,1)}, u32[]{:S(2)}) copy-start(bf16[256]{0:T(256)(128)(2,1)} %param.27) | copy-start | bytes 1540
  32.4 21.9 %copy-start.10 = (bf16[3,512]{1,0:T(4,128)(2,1)S(1)}, bf16[3,512]{1,0:T(4,128)(2,1)}, u32[]{:S(2)}) copy-start(bf16[3,512]{1,0:T(4,128)(2,1)} %param.19) | copy-start | bytes 9220
  42.4 23.5 %collective-permute-start.4 = (bf16[8,128,256]{2,1,0:T(8,128)(2,1)S(1)}, bf16[8,128,256]{2,1,0:T(8,128)(2,1)S(1)}, u32[]{:S(2)}, u32[]{:S(2)}) collective-permute-start(bf16[8,128,256]{2,1,0:T(8,128)(2,1)S(1)} %all_gather.11), channel_id=1, source_target_pairs={{0,2},{2,4},{4,6},{6,8},{8,10},{10,12},{12,14},{14,16},{16,18},{18... | collective-permute-start | bytes 1572872 | tf_op jit(solution)/shard_map/ppermute | solution.py:22
  42.4 28.7 %collective-permute-start.5 = (bf16[8,128,256]{2,1,0:T(8,128)(2,1)S(1)}, bf16[8,128,256]{2,1,0:T(8,128)(2,1)S(1)}, u32[]{:S(2)}, u32[]{:S(2)}) collective-permute-start(bf16[8,128,256]{2,1,0:T(8,128)(2,1)S(1)} %all_gather.11), channel_id=1, source_target_pairs={{2,0},{4,2},{6,4},{8,6},{10,8},{12,10},{14,12},{16,14},{18,16},{20... | collective-permute-start | bytes 1572872 | tf_op jit(solution)/shard_map/ppermute | solution.py:23
  54.3 17.0 %copy-start.3 = (bf16[256,256]{1,0:T(8,128)(2,1)S(1)}, bf16[256,256]{1,0:T(8,128)(2,1)}, u32[]{:S(2)}) copy-start(bf16[256,256]{1,0:T(8,128)(2,1)} %first.3) | copy-start | bytes 393220
  54.3 17.0 %copy-start.5 = (bf16[20,256]{1,0:T(8,128)(2,1)S(1)}, bf16[20,256]{1,0:T(8,128)(2,1)}, u32[]{:S(2)}) copy-start(bf16[20,256]{1,0:T(8,128)(2,1)} %filt.3) | copy-start | bytes 30724
  54.3 17.0 %copy-start.7 = (s32[4,4]{1,0:T(4,128)S(1)}, s32[4,4]{1,0:T(4,128)}, u32[]{:S(2)}) copy-start(s32[4,4]{1,0:T(4,128)} %pairs.3) | copy-start | bytes 196
  54.3 17.0 %copy-start.9 = (s32[4]{0:T(128)S(1)}, s32[4]{0:T(128)}, u32[]{:S(2)}) copy-start(s32[4]{0:T(128)} %counts.3) | copy-start | bytes 52
where the time goes:
time: 78.9 us; the launch traced here: 78.7 us
  waiting for transfers between devices  30 us (38%)
  starting transfers between devices  23.7 us (30%)
  Pallas kernels  15 us (19%)
  blocking collectives  6.65 us (8%)
  between operations  1.46 us (2%)
  other arithmetic  1.04 us (1%)
  local copies, waits for them, and re-layouts  0.87 us (1%)
    ppermute x3, waiting for transfers between devices, halo(): lax.ppermute(mine, 'box', [(i, (i + 1) % count) for i in range(count)])  22.9 us
    ppermute x3, starting transfers between devices, halo(): lax.ppermute(mine, 'box', [((i + 1) % count, i) for i in range(count)])  20.8 us
    pallas_call x1, Pallas kernels, shards(): pl.pallas_call(functools.partial(atom_kernel, tiles), out_shape=jax.Shape...  7.63 us
    pallas_call x1, Pallas kernels, shards(): pl.pallas_call(functools.partial(probe_kernel, tiles), out_shape=jax.Shap...  7.35 us
    ppermute x3, waiting for transfers between devices, halo(): lax.ppermute(mine, 'box', [((i + 1) % count, i) for i in range(count)])  7.08 us
    all_gather x3, blocking collectives, columns(): column = lax.all_gather(mine, 'tile', axis=0, tiled=True)  6.65 us
    ppermute x3, starting transfers between devices, halo(): lax.ppermute(mine, 'box', [(i, (i + 1) % count) for i in range(count)])  2.9 us
  transfers between devices with their start and end apart: 6, of which 4 were waited for; matrix products, arithmetic and copies ran while one was open for 1% of the time, Pallas kernels for 0%

commit v1 on v0

v1 whole, which is shorter than its diff:
```python
import functools
import math

import jax
import jax.numpy as jnp
from jax import lax
from jax.experimental import pallas as pl
from jax.experimental.pallas import tpu as pltpu
from jax.sharding import PartitionSpec as P

BLOCK = 128
CELL = 12.0
CUTOFF = 5.0
VMEM_LIMIT = 56 * 1024 * 1024
MESH = pl.DeviceIdType.MESH


def shifted_softplus(v):
    return jnp.maximum(v, 0.0) + jnp.log1p(jnp.exp(-jnp.abs(v))) - math.log(2.0)


def spread_filter(filt_ref, wide_ref):
    count = filt_ref.shape[0]
    mid = count // 2
    filt = filt_ref[...].astype(jnp.float32)
    for r in range(count):
        row = filt[r : r + 1, :] * math.exp(-0.5 * (r - mid) ** 2)
        wide_ref[r] = jnp.broadcast_to(row, wide_ref.shape[1:]).astype(jnp.bfloat16)


def basis_terms(tx, ty, tz, sx, sy, sz, count, limit, self_flag):
    dx, dy, dz = tx - sx, ty - sy, tz - sz
    square = dx * dx + dy * dy + dz * dz
    inside = square < limit
    if self_flag is not None:
        rows = lax.broadcasted_iota(jnp.int32, square.shape, 0)
        cols = lax.broadcasted_iota(jnp.int32, square.shape, 1)
        inside = jnp.logical_and(inside, rows - cols != self_flag)
    square = jnp.minimum(square, CUTOFF * CUTOFF)
    angle = square * (math.pi / (2.0 * CUTOFF)) ** 2
    cosine = jnp.full_like(angle, 1.0 / math.factorial(12))
    for n in (10, 8, 6, 4, 2, 0):
        cosine = cosine * angle + (-1.0) ** (n // 2) / math.factorial(n)
    mid = count // 2
    ratio = jnp.sqrt(square) * ((count - 1) / CUTOFF) - mid
    middle = jnp.where(inside, cosine * cosine * jnp.exp(-0.5 * ratio * ratio), 0.0)
    up, down = jnp.exp(ratio), jnp.exp(-ratio)
    terms = [None] * count
    terms[mid] = middle
    for r in range(mid + 1, count):
        terms[r] = terms[r - 1] * up
    for r in range(mid - 1, -1, -1):
        terms[r] = terms[r + 1] * down
    return [t.astype(jnp.bfloat16) for t in terms]


class Flow:
    def __init__(self, place, table, cell_rows, chunk_rows, sems):
        self.place, self.table, self.sems = place, table, sems
        self.cell_rows, self.chunk_rows = cell_rows, chunk_rows

    def rows(self, column, chunk):
        _, tile, _, tiles = self.place
        start = (column * tiles + tile) * self.cell_rows + chunk * self.chunk_rows
        return self.table.at[pl.ds(start, self.chunk_rows)]

    def copy(self, source, column, chunk, kind, box, tile):
        return pltpu.make_async_remote_copy(
            src_ref=source,
            dst_ref=self.rows(column, chunk),
            send_sem=self.sems.at[0, kind, chunk],
            recv_sem=self.sems.at[1, kind, chunk],
            device_id=(box, tile),
            device_id_type=MESH,
        )

    def copies(self, chunk, source=None):
        box, tile, boxes, tiles = self.place
        odd = lax.rem(box, 2)
        partner = box + 1 - 2 * odd
        onward = lax.rem(box + 2 - 4 * odd + boxes, boxes)
        from_partner, from_far = 2 - 2 * odd, 2 * odd
        source = self.rows(1, chunk) if source is None else source
        stages = [
            [self.copy(source, from_far, chunk, 0, partner, tile)],
            [self.copy(self.rows(from_partner, chunk), from_far, chunk, 1, onward, tile)],
            [],
        ]
        columns = [1, from_partner, from_far]
        for n in range(1, tiles):
            other = lax.rem(tile + n, tiles)
            for stage in range(3):
                origin = source if stage == 0 else self.rows(columns[stage], chunk)
                kind = 2 + stage * (tiles - 1) + n - 1
                stages[stage].append(
                    self.copy(origin, columns[stage], chunk, kind, box, other)
                )
        return stages

    def begin(self, chunk, source=None):
        for copy in self.copies(chunk, source)[0]:
            copy.start()

    def pass_partner(self, chunk, source=None):
        stages = self.copies(chunk, source)
        stages[0][0].wait_recv()
        for copy in stages[1]:
            copy.start()

    def pass_far(self, chunk, source=None):
        stages = self.copies(chunk, source)
        stages[1][0].wait_recv()
        for copy in stages[2]:
            copy.start()

    def finish(self, chunk, source=None):
        stages = self.copies(chunk, source)
        for copy in stages[0][1:] + stages[1][1:] + stages[2]:
            copy.wait_recv()

    def drain(self, chunk, source=None):
        for stage in self.copies(chunk, source):
            for copy in stage:
                copy.wait_send()


def greet(place):
    box, tile, boxes, tiles = place
    odd = lax.rem(box, 2)
    barrier = pltpu.get_barrier_semaphore()
    for near in (box + 1 - 2 * odd, lax.rem(box + 2, boxes), lax.rem(box + boxes - 2, boxes)):
        pl.semaphore_signal(barrier, inc=1, device_id=(near, tile), device_id_type=MESH)
    for n in range(1, tiles):
        pl.semaphore_signal(
            barrier, inc=1, device_id=(box, lax.rem(tile + n, tiles)), device_id_type=MESH
        )
    return lambda: pl.semaphore_wait(barrier, 3 + tiles - 1)


def kernel(
    boxes,
    tiles,
    atom_pairs,
    atom_counts,
    probe_pairs,
    probe_counts,
    probe_slab,
    own_pos,
    probe_pos,
    own,
    filt_atom,
    first,
    second,
    filt_probe,
    read_first,
    read_out,
    out,
    density,
    pos,
    feat,
    fresh,
    columns,
    atom_basis,
    probe_basis,
    wide_atom,
    wide_probe,
    pos_sems,
    feat_sems,
    fresh_sems,
):
    box, tile = lax.axis_index("box"), lax.axis_index("tile")
    place = (box, tile, boxes, tiles)
    blocks, most = atom_pairs.shape
    points, least = probe_pairs.shape
    count, _, width = wide_atom.shape
    ready = greet(place)

    own_rows = (tiles + tile) * blocks
    spread_filter(filt_atom, wide_atom)
    spread_filter(filt_probe, wide_probe)
    for part, targets in ((0, own_pos), (blocks, probe_pos)):

        def lay(block, carry, part=part, targets=targets):
            rows = targets[block]
            for n in range(3):
                columns[part + block, n] = jnp.broadcast_to(rows[n : n + 1], (BLOCK, BLOCK)).T
            return carry

        lax.fori_loop(0, targets.shape[0], lay, 0)
    pos[pl.ds(own_rows, blocks)] = own_pos[...]
    feat[pl.ds(own_rows, blocks)] = own[...]

    def locate(q, slab):
        cell = q // blocks
        step_x, step_z = cell // 3, lax.rem(cell, 3)
        near = lax.rem(slab + step_z + (tiles - 1), tiles)
        where = (step_x * tiles + near) * blocks + lax.rem(q, blocks)
        return where, step_x, step_z

    def basis(pair, pairs, counts, slab, part, store, self_check):
        block, k = pair // pairs.shape[1], lax.rem(pair, pairs.shape[1])
        q = pairs[block, k]
        where, step_x, step_z = locate(q, slab)
        shift_x = (step_x - 1).astype(jnp.float32) * CELL
        shift_z = (step_z - 1).astype(jnp.float32) * CELL
        limit = jnp.where(k < counts[block], CUTOFF * CUTOFF, -1.0)
        flag = jnp.where(q == 4 * blocks + block, 0, 2 * BLOCK) if self_check else None
        spot = pos[where]
        terms = basis_terms(
            columns[part + block, 0],
            columns[part + block, 1],
            columns[part + block, 2],
            spot[0:1, :] + shift_x,
            spot[1:2, :],
            spot[2:3, :] + shift_z,
            count,
            limit,
            flag,
        )
        for r in range(count):
            store[pair, :, r * BLOCK : (r + 1) * BLOCK] = terms[r]

    def messages(block, pairs, slab, table, wide, store):
        total = None
        for k in range(pairs.shape[1]):
            where, _, _ = locate(pairs[block, k], slab)
            source = table[where].reshape(BLOCK // 16, 16, width)
            scaled = [(source * wide[r][None]).reshape(BLOCK, width) for r in range(count)]
            part = jnp.dot(
                store[block * pairs.shape[1] + k],
                jnp.concatenate(scaled, axis=0),
                preferred_element_type=jnp.float32,
            )
            total = part if total is None else total + part
        return total.astype(jnp.bfloat16)

    def loop(start, stop, body):
        def step(n, carry):
            body(n)
            return carry

        lax.fori_loop(start, stop, step, 0)

    def atom_basis_of(pair):
        basis(pair, atom_pairs, atom_counts, tile, 0, atom_basis, True)

    def probe_basis_of(pair):
        basis(pair, probe_pairs, probe_counts, probe_slab[0], blocks, probe_basis, False)

    pos_flow = Flow(place, pos, blocks, blocks, pos_sems)
    feat_flow = Flow(place, feat, blocks, 1, feat_sems)
    fresh_flow = Flow(place, fresh, blocks, 1, fresh_sems)

    ready()
    pos_flow.begin(0)
    loop(0, blocks, feat_flow.begin)
    pos_flow.pass_partner(0)
    pos_flow.pass_far(0)
    pos_flow.finish(0)

    share = most // 2

    def pass_on_partner(chunk):
        feat_flow.pass_partner(chunk)
        loop(chunk * share, (chunk + 1) * share, atom_basis_of)

    def pass_on_far(chunk):
        feat_flow.pass_far(chunk)
        loop((blocks + chunk) * share, (blocks + chunk + 1) * share, atom_basis_of)

    loop(0, blocks, pass_on_partner)
    loop(0, blocks, pass_on_far)
    loop(2 * blocks * share, blocks * most, atom_basis_of)
    loop(0, blocks, feat_flow.finish)

    def update(block):
        total = messages(block, atom_pairs, tile, feat, wide_atom, atom_basis)
        hidden = shifted_softplus(
            jnp.dot(total, first[...], preferred_element_type=jnp.float32)
        ).astype(jnp.bfloat16)
        change = jnp.dot(hidden, second[...], preferred_element_type=jnp.float32)
        changed = (own[block].astype(jnp.float32) + change).astype(jnp.bfloat16)
        out[block] = changed
        fresh[own_rows + block] = changed
        fresh_flow.begin(block)

        @pl.when(block > 0)
        def _():
            fresh_flow.pass_partner(block - 1)

    loop(0, blocks, update)
    fresh_flow.pass_partner(blocks - 1)
    each = (points * least) // blocks

    def pass_on_fresh(chunk):
        fresh_flow.pass_far(chunk)
        loop(chunk * each, (chunk + 1) * each, probe_basis_of)

    loop(0, blocks, pass_on_fresh)
    loop(blocks * each, points * least, probe_basis_of)
    loop(0, blocks, fresh_flow.finish)

    def read(block):
        total = messages(block, probe_pairs, probe_slab[0], fresh, wide_probe, probe_basis)
        hidden = shifted_softplus(
            jnp.dot(total, read_first[...], preferred_element_type=jnp.float32)
        ).astype(jnp.bfloat16)
        lifted = hidden.astype(jnp.float32) * read_out[...].astype(jnp.float32)
        density[block] = jnp.sum(lifted.T, axis=0, keepdims=True)

    loop(0, points, read)
    pos_flow.drain(0)
    loop(0, blocks, feat_flow.drain)
    loop(0, blocks, fresh_flow.drain)


def shards(
    tiles,
    boxes,
    atom_pos,
    atom_feat,
    tile_cells,
    atom_pairs,
    atom_counts,
    probe_pos,
    probe_pairs,
    probe_counts,
    filt_atom,
    upd_first,
    upd_second,
    filt_probe,
    read_first,
    read_out,
):
    atoms, width = atom_feat.shape
    nb = atoms // BLOCK
    count = filt_atom.shape[0]
    points = probe_pairs.shape[0]
    rows = 3 * tiles * nb
    kinds = 2 + 3 * (tiles - 1)

    def blocks_of(pos):
        laid = pos.reshape(3, -1, BLOCK).transpose(1, 0, 2).astype(jnp.float32)
        return jnp.pad(laid, ((0, 0), (0, 5), (0, 0)))

    smem = pl.BlockSpec(memory_space=pltpu.SMEM)
    vmem = pl.BlockSpec(memory_space=pltpu.VMEM)
    fresh, density = pl.pallas_call(
        functools.partial(kernel, boxes, tiles),
        out_shape=(
            jax.ShapeDtypeStruct((nb, BLOCK, width), jnp.bfloat16),
            jax.ShapeDtypeStruct((points, 1, BLOCK), jnp.float32),
        ),
        in_specs=[smem] * 5 + [vmem] * 9,
        out_specs=(vmem, vmem),
        scratch_shapes=[
            pltpu.VMEM((rows, 8, BLOCK), jnp.float32),
            pltpu.VMEM((rows, BLOCK, width), jnp.bfloat16),
            pltpu.VMEM((rows, BLOCK, width), jnp.bfloat16),
            pltpu.VMEM((nb + points, 3, BLOCK, BLOCK), jnp.float32),
            pltpu.VMEM((nb * atom_pairs.shape[1], BLOCK, count * BLOCK), jnp.bfloat16),
            pltpu.VMEM((points * probe_pairs.shape[1], BLOCK, count * BLOCK), jnp.bfloat16),
            pltpu.VMEM((count, 16, width), jnp.bfloat16),
            pltpu.VMEM((count, 16, width), jnp.bfloat16),
            pltpu.SemaphoreType.DMA((2, kinds, 1)),
            pltpu.SemaphoreType.DMA((2, kinds, nb)),
            pltpu.SemaphoreType.DMA((2, kinds, nb)),
        ],
        compiler_params=pltpu.CompilerParams(
            collective_id=0, has_side_effects=True, vmem_limit_bytes=VMEM_LIMIT
        ),
    )(
        atom_pairs,
        atom_counts,
        probe_pairs,
        probe_counts,
        tile_cells,
        blocks_of(atom_pos),
        blocks_of(probe_pos),
        atom_feat.reshape(nb, BLOCK, width),
        filt_atom,
        upd_first,
        upd_second,
        filt_probe,
        read_first,
        read_out.reshape(1, width),
    )
    return (fresh.reshape(atoms, width), density.reshape(-1))


def solution(mesh):
    both = ("box", "tile")
    placed = (
        P(None, both),
        P(both, None),
        P(both),
        P(both, None),
        P(both),
        P(None, both),
        P(both, None),
        P(both),
    ) + (P(),) * 6
    return jax.shard_map(
        functools.partial(shards, mesh.shape["tile"], mesh.shape["box"]),
        mesh=mesh,
        in_specs=placed,
        out_specs=(P(both, None), P(both)),
        check_vma=False,
    )
```

time: 78.9 us -> 49.4 us (0.63)
  waiting for transfers between devices: 30 us -> 0 us
  Pallas kernels: 15 us -> 44.3 us
  starting transfers between devices: 23.7 us -> 0 us
  blocking collectives: 6.65 us -> 0 us
  local copies, waits for them, and re-layouts: 0.87 us -> 2.93 us
    ppermute x6 -> x0, waiting for transfers between devices: 30 us -> none  [the longest x3 22.9 us: halo(): lax.ppermute(mine, 'box', [(i, (i + 1) % count) for i in range(count)])]
    pallas_call x2 -> x1, Pallas kernels: 15 us -> 44.3 us  [shards(): pl.pallas_call(functools.partial(kernel, boxes, tiles), out_shape=(jax.Sh...]
    ppermute x6 -> x0, starting transfers between devices: 23.7 us -> none  [the longest x3 20.8 us: halo(): lax.ppermute(mine, 'box', [((i + 1) % count, i) for i in range(count)])]
    all_gather x3 -> x0, blocking collectives: 6.65 us -> none  [columns(): column = lax.all_gather(mine, 'tile', axis=0, tiled=True)]
    unnamed x26 -> x10, local copies, waits for them, and re-layouts: 0.86 us -> 2.36 us
  transfers between devices with their start and end apart: 6 -> 0, of which waited for: 4 -> 0; matrix products, arithmetic and copies ran while one was open for 1% -> 0% of each run, Pallas kernels for 0% -> 0%
where the time goes in v1:
time: 49.4 us; the launch traced here: 49.2 us
  Pallas kernels  44.3 us (90%)
  local copies, waits for them, and re-layouts  2.93 us (6%)
  between operations  1.35 us (3%)
  other arithmetic  0.61 us (1%)
    pallas_call x1, Pallas kernels, shards(): pl.pallas_call(functools.partial(kernel, boxes, tiles), out_shape=(jax.Sh...  44.3 us
    unnamed x10, local copies, waits for them, and re-layouts  2.36 us

profile of v1, /device:TPU:0, one launch (start us, length us, event | category | flops | bytes accessed | tf_op | source)
XLA Modules:
  0.0 49.2 jit_solution(3170374272124742768)
XLA Ops:
  0.6 0.0 copy-start.3
  0.6 0.0 copy-start.1
  1.3 0.0 copy-start
  1.3 0.0 copy-done.3
  1.3 0.6 %reshape.23.read_out = bf16[1,256]{1,0:T(2,128)(2,1)} reshape(bf16[256]{0:T(256)(128)(2,1)S(1)} %copy-done.3) | data formatting | bytes 1024 | tf_op jit(solution)/shard_map/reshape | solution.py:386
  1.9 0.0 copy-done.1
  1.9 0.1 copy-done
  2.0 0.6 %pad_convert_fusion = (f32[4,8,128]{2,1,0:T(8,128)}, f32[4,8,128]{2,1,0:T(8,128)}) fusion(bf16[4,3,128]{2,1,0:T(4,128)(2,1)S(1)} %bitcast.11, bf16[4,3,128]{2,1,0:T(4,128)(2,1)S(1)} %bitcast.12), kind=kLoop, calls=%fused_computation | loop fusion | flops 8192 | bytes 38912 | tf_op jit(solution)/shard_map/jit(_pad)/pad | solution.py:344
  2.6 44.3 %shard_map.149 = (bf16[4,128,256]{2,1,0:T(8,128)(2,1)}, f32[4,1,128]{2,1,0:T(1,128)}) custom-call(s32[4,6]{1,0:T(4,128)} %atom_pairs.1, s32[4]{0:T(128)} %atom_counts.1, s32[4,4]{1,0:T(4,128)} %probe_pairs.1, s32[4]{0:T(128)} %probe_counts.1, s32[1]{0:T(128)S(6)} %copy.18.probe_slab, f32[4,8,128]{2,1,0:T(8,128)} %get-tuple-element.7.own_pos, ...), custom_call_target="tpu_custom_call" | custom-call | tf_op jit(solution)/shard_map/pallas_call | solution.py:348
  46.9 0.0 copy-start.2
  46.9 1.7 %copy.19 = bf16[512,256]{1,0:T(8,128)(2,1)} copy(bf16[512,256]{1,0:T(8,128)(2,1)} %bitcast.10) | data formatting | bytes 524288
  48.6 0.0 copy-done.2
  48.6 0.6 %copy.20 = f32[512]{0:T(512)} copy(f32[512]{0:T(512)S(1)} %bitcast.13) | data formatting | bytes 4096
Async XLA Ops:
  0.6 0.7 %copy-start.3 = (bf16[256]{0:T(256)(128)(2,1)S(1)}, bf16[256]{0:T(256)(128)(2,1)}, u32[]{:S(2)}) copy-start(bf16[256]{0:T(256)(128)(2,1)} %param.27) | copy-start | bytes 1540
  0.6 1.3 %copy-start.1 = (bf16[3,512]{1,0:T(4,128)(2,1)S(1)}, bf16[3,512]{1,0:T(4,128)(2,1)}, u32[]{:S(2)}) copy-start(bf16[3,512]{1,0:T(4,128)(2,1)} %param.14) | copy-start | bytes 9220
  1.3 0.7 %copy-start = (bf16[3,512]{1,0:T(4,128)(2,1)S(1)}, bf16[3,512]{1,0:T(4,128)(2,1)}, u32[]{:S(2)}) copy-start(bf16[3,512]{1,0:T(4,128)(2,1)} %param.19) | copy-start | bytes 9220
  46.9 1.7 %copy-start.2 = (f32[4,1,128]{2,1,0:T(1,128)S(1)}, f32[4,1,128]{2,1,0:T(1,128)}, u32[]{:S(2)}) copy-start(f32[4,1,128]{2,1,0:T(1,128)} %get-tuple-element.5) | copy-start | bytes 6148

commit v2 on v1

--- a/solution.py
+++ b/solution.py
@@ -16,7 +16,7 @@
 
 
 def shifted_softplus(v):
-    return jnp.maximum(v, 0.0) + jnp.log1p(jnp.exp(-jnp.abs(v))) - math.log(2.0)
+    return jnp.maximum(v, 0.0) + jnp.log(1.0 + jnp.exp(-jnp.abs(v))) - math.log(2.0)
 
 
 def spread_filter(filt_ref, wide_ref):
@@ -126,15 +126,41 @@
 
 def greet(place):
     box, tile, boxes, tiles = place
-    odd = lax.rem(box, 2)
     barrier = pltpu.get_barrier_semaphore()
-    for near in (box + 1 - 2 * odd, lax.rem(box + 2, boxes), lax.rem(box + boxes - 2, boxes)):
-        pl.semaphore_signal(barrier, inc=1, device_id=(near, tile), device_id_type=MESH)
-    for n in range(1, tiles):
-        pl.semaphore_signal(
-            barrier, inc=1, device_id=(box, lax.rem(tile + n, tiles)), device_id_type=MESH
+    met = [(lax.rem(box + 2, boxes), tile), (lax.rem(box + boxes - 2, boxes), tile)]
+    met += [near for _, _, near in around(place)]
+    for near in met:
+        pl.semaphore_signal(barrier, inc=1, device_id=near, device_id_type=MESH)
+    return lambda: pl.semaphore_wait(barrier, len(met))
+
+
+def around(place):
+    box, tile, boxes, tiles = place
+    return [
+        (step, n, (lax.rem(box + step + boxes, boxes), lax.rem(tile + n, tiles)))
+        for step in (-1, 1, 0)
+        for n in range(tiles)
+        if step != 0 or n > 0
+    ]
+
+
+def send_positions(place, table, rows, sems):
+    _, tile, _, tiles = place
+    copies = []
+    for step, n, near in around(place):
+        kind = (step + 1) * tiles + n
+        copies.append(
+            pltpu.make_async_remote_copy(
+                src_ref=table.at[pl.ds((tiles + tile) * rows, rows)],
+                dst_ref=table.at[pl.ds(((1 - step) * tiles + tile) * rows, rows)],
+                send_sem=sems.at[0, kind],
+                recv_sem=sems.at[1, kind],
+                device_id=near,
+                device_id_type=MESH,
+            )
         )
-    return lambda: pl.semaphore_wait(barrier, 3 + tiles - 1)
+        copies[-1].start()
+    return copies
 
 
 def kernel(
@@ -176,18 +202,20 @@
     ready = greet(place)
 
     own_rows = (tiles + tile) * blocks
-    spread_filter(filt_atom, wide_atom)
-    spread_filter(filt_probe, wide_probe)
-    for part, targets in ((0, own_pos), (blocks, probe_pos)):
-
-        def lay(block, carry, part=part, targets=targets):
-            rows = targets[block]
+    def prepare():
+        spread_filter(filt_atom, wide_atom)
+        spread_filter(filt_probe, wide_probe)
+        for part, targets in ((0, own_pos), (blocks, probe_pos)):
             for n in range(3):
-                columns[part + block, n] = jnp.broadcast_to(rows[n : n + 1], (BLOCK, BLOCK)).T
-            return carry
-
-        lax.fori_loop(0, targets.shape[0], lay, 0)
-    pos[pl.ds(own_rows, blocks)] = own_pos[...]
+                row = targets[n : n + 1, :].astype(jnp.float32)
+                for block in range(targets.shape[1] // BLOCK):
+                    cut = row[:, block * BLOCK : (block + 1) * BLOCK]
+                    columns[part + block, n] = jnp.broadcast_to(cut, (BLOCK, BLOCK)).T
+
+    mine = own_pos[...].astype(jnp.float32)
+    for block in range(blocks):
+        pos[own_rows + block, 0:3, :] = mine[:, block * BLOCK : (block + 1) * BLOCK]
+        pos[own_rows + block, 3:8, :] = jnp.zeros((5, BLOCK), jnp.float32)
     feat[pl.ds(own_rows, blocks)] = own[...]
 
     def locate(q, slab):
@@ -247,30 +275,33 @@
     def probe_basis_of(pair):
         basis(pair, probe_pairs, probe_counts, probe_slab[0], blocks, probe_basis, False)
 
-    pos_flow = Flow(place, pos, blocks, blocks, pos_sems)
     feat_flow = Flow(place, feat, blocks, 1, feat_sems)
     fresh_flow = Flow(place, fresh, blocks, 1, fresh_sems)
 
+    prepare()
     ready()
-    pos_flow.begin(0)
+    sent = send_positions(place, pos, blocks, pos_sems)
     loop(0, blocks, feat_flow.begin)
-    pos_flow.pass_partner(0)
-    pos_flow.pass_far(0)
-    pos_flow.finish(0)
-
-    share = most // 2
-
-    def pass_on_partner(chunk):
-        feat_flow.pass_partner(chunk)
-        loop(chunk * share, (chunk + 1) * share, atom_basis_of)
-
-    def pass_on_far(chunk):
-        feat_flow.pass_far(chunk)
-        loop((blocks + chunk) * share, (blocks + chunk + 1) * share, atom_basis_of)
-
-    loop(0, blocks, pass_on_partner)
-    loop(0, blocks, pass_on_far)
-    loop(2 * blocks * share, blocks * most, atom_basis_of)
+    for copy in sent:
+        copy.wait_recv()
+
+    steps = blocks + 2
+    share = blocks * most // steps
+
+    def pass_on(n):
+        @pl.when(n < blocks)
+        def _():
+            feat_flow.pass_partner(n)
+
+        @pl.when(n >= 2)
+        def _():
+            feat_flow.pass_far(n - 2)
+
+        loop(n * share, (n + 1) * share, atom_basis_of)
+
+    loop(0, steps, pass_on)
+    if steps * share < blocks * most:
+        loop(steps * share, blocks * most, atom_basis_of)
     loop(0, blocks, feat_flow.finish)
 
     def update(block):
@@ -284,20 +315,24 @@
         fresh[own_rows + block] = changed
         fresh_flow.begin(block)
 
-        @pl.when(block > 0)
+        @pl.when(block >= 2)
         def _():
-            fresh_flow.pass_partner(block - 1)
+            fresh_flow.pass_partner(block - 2)
 
     loop(0, blocks, update)
-    fresh_flow.pass_partner(blocks - 1)
-    each = (points * least) // blocks
-
-    def pass_on_fresh(chunk):
-        fresh_flow.pass_far(chunk)
-        loop(chunk * each, (chunk + 1) * each, probe_basis_of)
+    each = points * least // blocks
+
+    def pass_on_fresh(n):
+        @pl.when(n < 2)
+        def _():
+            fresh_flow.pass_partner(blocks - 2 + n)
+
+        fresh_flow.pass_far(n)
+        loop(n * each, (n + 1) * each, probe_basis_of)
 
     loop(0, blocks, pass_on_fresh)
-    loop(blocks * each, points * least, probe_basis_of)
+    if blocks * each < points * least:
+        loop(blocks * each, points * least, probe_basis_of)
     loop(0, blocks, fresh_flow.finish)
 
     def read(block):
@@ -305,11 +340,15 @@
         hidden = shifted_softplus(
             jnp.dot(total, read_first[...], preferred_element_type=jnp.float32)
         ).astype(jnp.bfloat16)
-        lifted = hidden.astype(jnp.float32) * read_out[...].astype(jnp.float32)
-        density[block] = jnp.sum(lifted.T, axis=0, keepdims=True)
+        last = jnp.broadcast_to(read_out[...].reshape(1, width), (16, width))
+        summed = lax.dot_general(
+            last, hidden, (((1,), (1,)), ((), ())), preferred_element_type=jnp.float32
+        )
+        density[block] = summed[0:1, :]
 
     loop(0, points, read)
-    pos_flow.drain(0)
+    for copy in sent:
+        copy.wait_send()
     loop(0, blocks, feat_flow.drain)
     loop(0, blocks, fresh_flow.drain)
 
@@ -339,10 +378,6 @@
     rows = 3 * tiles * nb
     kinds = 2 + 3 * (tiles - 1)
 
-    def blocks_of(pos):
-        laid = pos.reshape(3, -1, BLOCK).transpose(1, 0, 2).astype(jnp.float32)
-        return jnp.pad(laid, ((0, 0), (0, 5), (0, 0)))
-
     smem = pl.BlockSpec(memory_space=pltpu.SMEM)
     vmem = pl.BlockSpec(memory_space=pltpu.VMEM)
     fresh, density = pl.pallas_call(
@@ -362,7 +397,7 @@
             pltpu.VMEM((points * probe_pairs.shape[1], BLOCK, count * BLOCK), jnp.bfloat16),
             pltpu.VMEM((count, 16, width), jnp.bfloat16),
             pltpu.VMEM((count, 16, width), jnp.bfloat16),
-            pltpu.SemaphoreType.DMA((2, kinds, 1)),
+            pltpu.SemaphoreType.DMA((2, 3 * tiles)),
             pltpu.SemaphoreType.DMA((2, kinds, nb)),
             pltpu.SemaphoreType.DMA((2, kinds, nb)),
         ],
@@ -375,8 +410,8 @@
         probe_pairs,
         probe_counts,
         tile_cells,
-        blocks_of(atom_pos),
-        blocks_of(probe_pos),
+        atom_pos,
+        probe_pos,
         atom_feat.reshape(nb, BLOCK, width),
         filt_atom,
         upd_first,

time: 49.4 us -> 49.2 us (level)
  other arithmetic: 0.61 us -> 0 us
  local copies, waits for them, and re-layouts: 2.93 us -> 3.47 us
    pad x1 -> x0, other arithmetic: 0.61 us -> none  [blocks_of(): return jnp.pad(laid, ((0, 0), (0, 5), (0, 0)))]
    unnamed x10 -> x6, local copies, waits for them, and re-layouts: 2.36 us -> 2.9 us
where the time goes in v2:
time: 49.2 us; the launch traced here: 49 us
  Pallas kernels  44.2 us (90%)
  local copies, waits for them, and re-layouts  3.47 us (7%)
  between operations  1.3 us (3%)
    pallas_call x1, Pallas kernels, shards(): pl.pallas_call(functools.partial(kernel, boxes, tiles), out_shape=(jax.Sh...  44.2 us
    unnamed x6, local copies, waits for them, and re-layouts  2.9 us

profile of v2, /device:TPU:0, one launch (start us, length us, event | category | flops | bytes accessed | tf_op | source)
XLA Modules:
  0.0 49.0 jit_solution(17032524681844811501)
XLA Ops:
  1.3 0.0 copy-start.1
  1.3 0.6 %copy-done.1 = bf16[256]{0:T(256)(128)(2,1)S(1)} copy-done((bf16[256]{0:T(256)(128)(2,1)S(1)}, bf16[256]{0:T(256)(128)(2,1)}, u32[]{:S(2)}) %copy-start.1) | copy-done | bytes 536
  1.9 0.6 %reshape.17.read_out = bf16[1,256]{1,0:T(2,128)(2,1)} reshape(bf16[256]{0:T(256)(128)(2,1)S(1)} %copy-done.1) | data formatting | bytes 1024 | tf_op jit(solution)/shard_map/reshape | solution.py:421
  2.5 44.2 %shard_map.149 = (bf16[4,128,256]{2,1,0:T(8,128)(2,1)}, f32[4,1,128]{2,1,0:T(1,128)}) custom-call(s32[4,6]{1,0:T(4,128)} %atom_pairs.1, s32[4]{0:T(128)} %atom_counts.1, s32[4,4]{1,0:T(4,128)} %probe_pairs.1, s32[4]{0:T(128)} %probe_counts.1, s32[1]{0:T(128)S(6)} %copy.18.probe_slab, bf16[3,512]{1,0:T(4,128)(2,1)} %own_pos.1, bf16[3,512]{1,0:T(4,128)(2,1)} %probe_pos.1, ...), custom_call_target="tpu_custom_call" | custom-call | tf_op jit(solution)/shard_map/pallas_call | solution.py:383
  46.7 0.0 copy-start
  46.7 1.7 %copy.19 = bf16[512,256]{1,0:T(8,128)(2,1)} copy(bf16[512,256]{1,0:T(8,128)(2,1)} %bitcast.4) | data formatting | bytes 524288
  48.4 0.0 copy-done
  48.4 0.6 %copy.20 = f32[512]{0:T(512)} copy(f32[512]{0:T(512)S(1)} %bitcast.5) | data formatting | bytes 4096
Async XLA Ops:
  1.3 0.7 %copy-start.1 = (bf16[256]{0:T(256)(128)(2,1)S(1)}, bf16[256]{0:T(256)(128)(2,1)}, u32[]{:S(2)}) copy-start(bf16[256]{0:T(256)(128)(2,1)} %param.27) | copy-start | bytes 1540
  46.7 1.7 %copy-start = (f32[4,1,128]{2,1,0:T(1,128)S(1)}, f32[4,1,128]{2,1,0:T(1,128)}, u32[]{:S(2)}) copy-start(f32[4,1,128]{2,1,0:T(1,128)} %get-tuple-element.5) | copy-start | bytes 6148
